TPU v7x, 32 devices: a whole 2x2x4 slice. The times are simulated.
32 devices in a mesh: groups: 2 (over x), dp: 16 (over z, y, core).
Axes of the slice: x: 2, y: 2, z: 4, core: 2. Of those that a mesh axis runs over, the one named last changes fastest.
Arguments:
- embeddings: bfloat16 [4096, 1024], P(('groups', 'dp')), parts along dimension 0
- cluster_ids: int32 [4096], P(('groups', 'dp')), parts along dimension 0, may hold values from 0 to 511, as said below
- owner: int32 [1024], P('groups'), parts along dimension 0, may hold values from 0 to 15, as said below
Outputs:
- smoothed: bfloat16 [4096, 1024], P(('groups', 'dp')), parts along dimension 0
There are 2 independent parts, one for each index of `groups`. A program takes and returns all parts, laid end to end along the dimension named above; each array names one. Nothing has to cross between parts.
Inputs may be any that keep to these rules, and one draw needn't show every extreme that they name: `owner`: every device number owns exactly 32 clusters. `cluster_ids`: among the rows of one device, at most 16 belong to clusters of one owner, and on every device some owner gets exactly 16 of them.
All inputs are finite; a program needn't handle non-finite values.
Results may differ from a plain program's by a relative error of at most 0.0041.
Values may be sent and summed in bfloat16 or wider, within the bound.
A program may use at most 64 MiB of HBM per device.

v0:
```python
import jax
import jax.numpy as jnp
from jax import lax
from jax.sharding import PartitionSpec as P

epsilon = 1e-06
sharpness_scale = 0.25


def normalize(rows):
    values = rows.astype(jnp.float32)
    return (values * lax.rsqrt(jnp.sum(values * values, axis=1, keepdims=True) + epsilon)).astype(
        jnp.bfloat16
    )


def kernel_terms(query_unit, query_labels, key_unit, compared_group_ids, key_rows):
    pairwise_similarity = jnp.dot(query_unit, key_unit.T, preferred_element_type=jnp.float32)
    shared_group_filter = (query_labels[:, None] == compared_group_ids[None, :]) & (
        query_labels[:, None] >= 0
    )
    affinity_factor = jnp.where(
        shared_group_filter,
        jnp.exp((pairwise_similarity - 1.0) / sharpness_scale),
        jnp.float32(0.0),
    )
    total = jnp.sum(affinity_factor, axis=1)
    numer = jnp.dot(
        affinity_factor.astype(jnp.bfloat16), key_rows, preferred_element_type=jnp.float32
    )
    return (numer, total)


def finish(numer, total, labels):
    total = jnp.where(labels >= 0, total, jnp.float32(1.0))
    return (numer / total[:, None]).astype(jnp.bfloat16)


def shards(embeddings, cluster_ids, owner):
    peers = lax.axis_size("dp")
    rows_dev, width = embeddings.shape
    slot = 2 * rows_dev // peers
    dest = jnp.take(owner, cluster_ids)
    onehot = (dest[:, None] == jnp.arange(peers, dtype=jnp.int32)[None, :]).astype(jnp.int32)
    rank = jnp.sum(onehot * (jnp.cumsum(onehot, axis=0) - 1), axis=1)
    target = dest * slot + rank
    outgoing = (
        jnp.zeros((peers * slot, width), jnp.bfloat16)
        .at[target]
        .set(embeddings)
        .reshape(peers, slot, width)
    )
    labels = (
        jnp.full((peers * slot,), -1, jnp.int32).at[target].set(cluster_ids).reshape(peers, slot)
    )
    received, got_labels = (
        lax.all_to_all(outgoing, "dp", split_axis=0, concat_axis=0, tiled=True),
        lax.all_to_all(labels, "dp", split_axis=0, concat_axis=0, tiled=True),
    )
    flat_rows = received.reshape(-1, width)
    flat_labels = got_labels.reshape(-1)
    unit = normalize(flat_rows)
    numer, total = kernel_terms(unit, flat_labels, unit, flat_labels, flat_rows)
    result = finish(numer, total, flat_labels).reshape(peers, slot, width)
    back = lax.all_to_all(result, "dp", split_axis=0, concat_axis=0, tiled=True)
    return back.reshape(-1, width)[target]


def solution(mesh):
    placed = (P(("groups", "dp"), None), P(("groups", "dp")), P("groups"))
    return jax.shard_map(
        shards, mesh=mesh, in_specs=placed, out_specs=P(("groups", "dp"), None), check_vma=False
    )
```

profile of v0, /device:TPU:0, one launch (start us, length us, event | category | flops | bytes accessed | tf_op | source)
XLA Modules:
  0.0 57.8 jit_solution(17104505909790052697)
XLA Ops:
  0.0 0.0 copy-start
  0.0 0.7 %compare_select_fusion.1 = s32[128]{0:T(128)S(1)} fusion(s32[128]{0:T(128)} %param.4), kind=kLoop, calls=%fused_computation.24 | loop fusion | flops 384 | bytes 1024 | tf_op jit(solution)/shard_map/jit(_take)/jit(_where)/select_n | solution.py:43
  0.7 0.0 copy-start.1
  0.7 1.3 %gather_fusion = s32[128]{0:T(128)S(1)} fusion(s32[512]{0:T(512)S(1)} %copy-done, s32[1024]{0:T(1024)S(1)} %pad_clamp_fusion.1), kind=kCustom, calls=%fused_computation | custom fusion | bytes 1536 | tf_op jit(solution)/shard_map/jit(_take)/gather | solution.py:43
  2.0 0.1 fusion.9
  2.1 0.2 reduce_window_sum.11
  2.3 0.2 select_reduce_fusion
  2.4 1.0 %scatter_custom_fusion = s32[256]{0:T(256)S(1)} fusion(s32[128]{0:T(128)S(1)} %compare_select_fusion, s32[128]{0:T(128)S(1)} %copy-done.1, s32[]{:T(128)} %constant.13.clone.1), kind=kCustom, calls=%fused_computation.28 | custom fusion | bytes 1028 | tf_op jit(solution)/shard_map/scatter | solution.py:54
  3.4 0.7 %all_to_all.12 = s32[16,1,16]{2,1,0:T(1,128)} reshape(s32[256]{0:T(256)S(1)} %scatter_custom_fusion) | data formatting | bytes 2048 | tf_op jit(solution)/shard_map/all_to_all | solution.py:58
  4.1 7.4 %all-to-all-start = ((s32[16,1,16]{2,1,0:T(1,128)}), s32[16,1,16]{2,1,0:T(1,128)S(1)}, u32[]{:S(2)}, u32[]{:S(2)}) async-start(s32[16,1,16]{2,1,0:T(1,128)} %all_to_all.12), calls=%async_computation | async-start | bytes 16384 | tf_op jit(solution)/shard_map/all_to_all | solution.py:58
  11.5 2.4 %scatter_custom_fusion.1 = bf16[256,1024]{1,0:T(8,128)(2,1)} fusion(s32[128]{0:T(128)S(1)} %compare_select_fusion, bf16[128,1024]{1,0:T(8,128)(2,1)} %param.3, bf16[]{:T(256)} %constant.12.clone.1), kind=kCustom, calls=%fused_computation.14 | custom fusion | bytes 524800 | tf_op jit(solution)/shard_map/scatter | solution.py:50
  13.9 4.0 %all-to-all-done = s32[16,1,16]{2,1,0:T(1,128)S(1)} async-done(((s32[16,1,16]{2,1,0:T(1,128)}), s32[16,1,16]{2,1,0:T(1,128)S(1)}, u32[]{:S(2)}, u32[]{:S(2)}) %all-to-all-start) | async-done | bytes 1056 | tf_op jit(solution)/shard_map/all_to_all | solution.py:58
  17.8 3.6 %all-to-all-start.1 = ((bf16[16,16,1024]{2,1,0:T(8,128)(2,1)}), bf16[16,16,1024]{2,1,0:T(8,128)(2,1)S(1)}, u32[]{:S(2)}, u32[]{:S(2)}) async-start(bf16[16,16,1024]{2,1,0:T(8,128)(2,1)} %bitcast), calls=%async_computation.1 | async-start | bytes 1048576 | tf_op jit(solution)/shard_map/all_to_all | solution.py:57
  21.4 0.5 broadcast.66
  21.9 0.7 %reduce.4 = s32[16,16]{1,0:T(8,128)S(1)} reduce(s32[16,1,16]{2,1,0:T(1,128)S(1)} %all-to-all-done, s32[]{:T(128)} %broadcast.66), dimensions={1}, to_apply=%all_to_all.13.reduce_sub_computation.3 | reduce | bytes 2052 | tf_op jit(solution)/shard_map/all_to_all | solution.py:58
  22.6 0.1 eq.31
  22.7 13.1 %all-to-all-done.1 = bf16[16,16,1024]{2,1,0:T(8,128)(2,1)S(1)} async-done(((bf16[16,16,1024]{2,1,0:T(8,128)(2,1)}), bf16[16,16,1024]{2,1,0:T(8,128)(2,1)S(1)}, u32[]{:S(2)}, u32[]{:S(2)}) %all-to-all-start.1) | async-done | bytes 524320 | tf_op jit(solution)/shard_map/all_to_all | solution.py:57
  35.9 0.2 fusion.4
  36.0 0.2 fusion.5
  36.2 0.4 fusion.12
  36.6 1.1 %fusion = bf16[256,1024]{1,0:T(8,128)(2,1)} fusion(bf16[256,1024]{1,0:T(8,128)(2,1)S(1)} %bitcast.10, f32[256]{0:T(256)S(1)} %broadcast_select_fusion, bf16[256,256]{0,1:T(8,128)(2,1)S(1)} %get-tuple-element.6), kind=kOutput, calls=%fused_computation.7 | convolution fusion | flops 134742016 | bytes 1180672 | tf_op jit(solution)/shard_map/dot_general | solution.py:28
  37.7 4.0 %all-to-all-start.2 = ((bf16[16,16,1024]{2,1,0:T(8,128)(2,1)}), bf16[16,16,1024]{2,1,0:T(8,128)(2,1)S(1)}, u32[]{:S(2)}, u32[]{:S(2)}) async-start(bf16[16,16,1024]{2,1,0:T(8,128)(2,1)} %bitcast.3), calls=%async_computation.2 | async-start | bytes 1048576 | tf_op jit(solution)/shard_map/all_to_all | solution.py:65
  41.8 14.5 %all-to-all-done.2 = bf16[16,16,1024]{2,1,0:T(8,128)(2,1)S(1)} async-done(((bf16[16,16,1024]{2,1,0:T(8,128)(2,1)}), bf16[16,16,1024]{2,1,0:T(8,128)(2,1)S(1)}, u32[]{:S(2)}, u32[]{:S(2)}) %all-to-all-start.2) | async-done | bytes 524320 | tf_op jit(solution)/shard_map/all_to_all | solution.py:65
  56.2 1.6 %gather_fusion.1 = bf16[128,1024]{1,0:T(8,128)(2,1)} fusion(bf16[256,1024]{1,0:T(8,128)(2,1)S(1)} %bitcast.9, s32[1024]{0:T(1024)S(1)} %pad_clamp_fusion), kind=kCustom, calls=%fused_computation.1 | custom fusion | bytes 524800 | tf_op jit(solution)/shard_map/gather | solution.py:66
  (9 shorter events, 0.1 us)
Async XLA Ops:
  0.0 0.7 %copy-start = (s32[512]{0:T(512)S(1)}, s32[512]{0:T(512)}, u32[]{:S(2)}) copy-start(s32[512]{0:T(512)} %param.5) | copy-start | bytes 6148
  0.7 1.3 %copy-start.1 = (s32[128]{0:T(128)S(1)}, s32[128]{0:T(128)}, u32[]{:S(2)}) copy-start(s32[128]{0:T(128)} %param.4) | copy-start | bytes 1540
  4.1 13.7 %all-to-all-start = ((s32[16,1,16]{2,1,0:T(1,128)}), s32[16,1,16]{2,1,0:T(1,128)S(1)}, u32[]{:S(2)}, u32[]{:S(2)}) async-start(s32[16,1,16]{2,1,0:T(1,128)} %all_to_all.12), calls=%async_computation | async-start | bytes 16384 | tf_op jit(solution)/shard_map/all_to_all | solution.py:58
  17.8 18.0 %all-to-all-start.1 = ((bf16[16,16,1024]{2,1,0:T(8,128)(2,1)}), bf16[16,16,1024]{2,1,0:T(8,128)(2,1)S(1)}, u32[]{:S(2)}, u32[]{:S(2)}) async-start(bf16[16,16,1024]{2,1,0:T(8,128)(2,1)} %bitcast), calls=%async_computation.1 | async-start | bytes 1048576 | tf_op jit(solution)/shard_map/all_to_all | solution.py:57
  37.7 18.5 %all-to-all-start.2 = ((bf16[16,16,1024]{2,1,0:T(8,128)(2,1)}), bf16[16,16,1024]{2,1,0:T(8,128)(2,1)S(1)}, u32[]{:S(2)}, u32[]{:S(2)}) async-start(bf16[16,16,1024]{2,1,0:T(8,128)(2,1)} %bitcast.3), calls=%async_computation.2 | async-start | bytes 1048576 | tf_op jit(solution)/shard_map/all_to_all | solution.py:65
where the time goes:
time: 58.2 us; the launch traced here: 57.8 us
  waiting for transfers between devices  31.6 us (54%)
  starting transfers between devices  15 us (26%)
  local copies, waits for them, and re-layouts  7.47 us (13%)
  other arithmetic  2.15 us (4%)
  matrix products  1.49 us (3%)
    all_to_all x1, waiting for transfers between devices, shards(): back = lax.all_to_all(result, 'dp', split_axis=0, concat_axis=0, tiled=True)  14.5 us
    all_to_all x1, waiting for transfers between devices, shards(): lax.all_to_all(outgoing, 'dp', split_axis=0, concat_axis=0, tiled=True)  13.1 us
    all_to_all x1, starting transfers between devices, shards(): lax.all_to_all(labels, 'dp', split_axis=0, concat_axis=0, tiled=True)  7.39 us
    all_to_all x1, starting transfers between devices, shards(): back = lax.all_to_all(result, 'dp', split_axis=0, concat_axis=0, tiled=True)  4.02 us
    all_to_all x1, waiting for transfers between devices, shards(): lax.all_to_all(labels, 'dp', split_axis=0, concat_axis=0, tiled=True)  3.96 us
    all_to_all x1, starting transfers between devices, shards(): lax.all_to_all(outgoing, 'dp', split_axis=0, concat_axis=0, tiled=True)  3.57 us
    scatter x1, local copies, waits for them, and re-layouts, shards(): outgoing = jnp.zeros((peers * slot, width), jnp.bfloat16).at[target].set(...  2.37 us
    gather x1, local copies, waits for them, and re-layouts, shards(): return back.reshape(-1, width)[target]  1.56 us
  transfers between devices with their start and end apart: 3, of which 3 were waited for; matrix products, arithmetic and copies ran while one was open for 6% of the time, Pallas kernels for 0%

commit v1 on v0

--- a/solution.py
+++ b/solution.py
@@ -1,10 +1,15 @@
+import functools
+
 import jax
 import jax.numpy as jnp
 from jax import lax
+from jax.experimental import pallas as pl
+from jax.experimental.pallas import tpu as pltpu
 from jax.sharding import PartitionSpec as P
 
 epsilon = 1e-06
 sharpness_scale = 0.25
+ROW_TILE = 16
 
 
 def normalize(rows):
@@ -36,7 +41,7 @@
     return (numer / total[:, None]).astype(jnp.bfloat16)
 
 
-def shards(embeddings, cluster_ids, owner):
+def by_collectives(embeddings, cluster_ids, owner):
     peers = lax.axis_size("dp")
     rows_dev, width = embeddings.shape
     slot = 2 * rows_dev // peers
@@ -66,6 +71,172 @@
     return back.reshape(-1, width)[target]
 
 
+def iota(shape, axis):
+    return lax.broadcasted_iota(jnp.int32, shape, axis)
+
+
+def smooth_kernel(
+    peers, slot, emb_hbm, ids_ref, owner_ref, out_ref,
+    emb, sent, got, unit, made, back, place, lab_out, lab_in,
+    emb_sem, lab_send, lab_recv, row_send, row_recv, back_send, back_recv,
+):
+    rows_dev, width = emb.shape
+    clusters = owner_ref.shape[1]
+    slots = peers * slot
+    me = lax.axis_index("dp")
+    load = pltpu.make_async_copy(emb_hbm, emb, emb_sem)
+    load.start()
+
+    barrier = pltpu.get_barrier_semaphore()
+    for k in range(1, peers):
+        pl.semaphore_signal(
+            barrier, inc=1, device_id={"dp": lax.rem(me + k, peers)},
+            device_id_type=pl.DeviceIdType.MESH,
+        )
+
+    order = sorted(range(1, peers), key=lambda k: abs(k - peers // 2))
+
+    def remote(src, dst, send, recv, k, forward):
+        peer = lax.rem(me + (k if forward else peers - k), peers)
+        return pltpu.make_async_remote_copy(
+            src_ref=src, dst_ref=dst, send_sem=send.at[k], recv_sem=recv.at[k],
+            device_id={"dp": peer}, device_id_type=pl.DeviceIdType.MESH,
+        )
+
+    def block(ref, k):
+        return ref.at[pl.ds(k * slot, slot)]
+
+    lab_copy = {
+        k: remote(lab_out, lab_in.at[k], lab_send, lab_recv, k, True) for k in order
+    }
+    row_copy = {
+        k: remote(block(sent, k), block(got, k), row_send, row_recv, k, True) for k in order
+    }
+    back_copy = {
+        k: remote(block(made, k), block(back, k), back_send, back_recv, k, False) for k in order
+    }
+
+    ids = ids_ref[...]
+    which = (iota((clusters, rows_dev), 0) == ids).astype(jnp.bfloat16)
+    owners = jnp.broadcast_to(owner_ref[...].astype(jnp.bfloat16), (8, clusters))
+    dest = jnp.dot(owners, which, preferred_element_type=jnp.float32)[:1].astype(jnp.int32)
+    ahead = dest - me
+    ahead = jnp.where(ahead < 0, ahead + peers, ahead)
+    hit = iota((peers, rows_dev), 0) == ahead
+    earlier = (iota((rows_dev, rows_dev), 0) < iota((rows_dev, rows_dev), 1)).astype(jnp.bfloat16)
+    count = jnp.dot(hit.astype(jnp.bfloat16), earlier, preferred_element_type=jnp.float32)
+    rank = jnp.sum(jnp.where(hit, count, 0.0), axis=0, keepdims=True).astype(jnp.int32)
+    target = ahead * slot + rank
+    put = (iota((slots, rows_dev), 0) == target).astype(jnp.bfloat16)
+    place[...] = put
+
+    row8 = iota((8, rows_dev), 0)
+    high = ids // 64
+    parts = jnp.where(row8 == 0, high, jnp.where(row8 == 1, ids - 64 * high, 1))
+    spread = lax.dot_general(
+        parts.astype(jnp.bfloat16), put, (((1,), (1,)), ((), ())),
+        preferred_element_type=jnp.float32,
+    )
+    labels = (64.0 * spread[0:1] + spread[1:2] + (spread[2:3] - 1.0)).astype(jnp.int32)
+    lab_out[...] = labels
+    lab_in[0] = labels
+
+    far = slice(slots // 4, 3 * slots // 4)
+    groups = [far, slice(0, slots // 4), slice(3 * slots // 4, slots)]
+
+    def inside(part):
+        return [k for k in order if part.start <= k * slot < part.stop]
+
+    load.wait()
+    pl.semaphore_wait(barrier, peers - 1)
+    for k in order:
+        lab_copy[k].start()
+    for part in groups:
+        sent[part, :] = jnp.dot(
+            place[part, :], emb[...], preferred_element_type=jnp.float32
+        ).astype(jnp.bfloat16)
+        for k in inside(part):
+            row_copy[k].start()
+    got[:slot, :] = sent[:slot, :]
+    unit[:slot, :] = normalize(got[:slot, :])
+
+    for k in order:
+        lab_copy[k].wait_recv()
+    lane = iota((1, slots), 1)
+    label_row = lab_in[0]
+    for k in range(1, peers):
+        label_row = jnp.where(lane >= k * slot, lab_in[k], label_row)
+    square = iota((slots, slots), 0) == iota((slots, slots), 1)
+    label_col = jnp.sum(jnp.where(square, label_row, 0), axis=1, keepdims=True)
+    same = label_col == label_row
+
+    for k in reversed(order):
+        row_copy[k].wait_recv()
+        here = slice(k * slot, (k + 1) * slot)
+        unit[here, :] = normalize(got[here, :])
+
+    gram = lax.dot_general(
+        unit[...], unit[...], (((1,), (1,)), ((), ())), preferred_element_type=jnp.float32
+    )
+    weight = jnp.where(same, jnp.exp((gram - 1.0) / sharpness_scale), 0.0)
+    total = jnp.sum(weight, axis=1, keepdims=True)
+    weight_b = weight.astype(jnp.bfloat16)
+    for part in groups:
+        numer = jnp.dot(weight_b[part], got[...], preferred_element_type=jnp.float32)
+        made[part, :] = (numer / total[part]).astype(jnp.bfloat16)
+        for k in inside(part):
+            back_copy[k].start()
+    back[:slot, :] = made[:slot, :]
+
+    for k in reversed(order):
+        back_copy[k].wait_recv()
+    out_ref[...] = lax.dot_general(
+        place[...], back[...], (((0,), (0,)), ((), ())), preferred_element_type=jnp.float32
+    ).astype(out_ref.dtype)
+    for k in order:
+        lab_copy[k].wait_send()
+        row_copy[k].wait_send()
+        back_copy[k].wait_send()
+
+
+def by_kernel(embeddings, cluster_ids, owner):
+    peers = lax.axis_size("dp")
+    rows_dev, width = embeddings.shape
+    slot = 2 * rows_dev // peers
+    slots = peers * slot
+    sems = pltpu.SemaphoreType.DMA((peers,))
+    vmem = pl.BlockSpec(memory_space=pltpu.VMEM)
+    return pl.pallas_call(
+        functools.partial(smooth_kernel, peers, slot),
+        out_shape=jax.ShapeDtypeStruct((rows_dev, width), jnp.bfloat16),
+        in_specs=[pl.BlockSpec(memory_space=pl.ANY), vmem, vmem],
+        out_specs=vmem,
+        scratch_shapes=[
+            pltpu.VMEM((rows_dev, width), jnp.bfloat16),
+            pltpu.VMEM((slots, width), jnp.bfloat16),
+            pltpu.VMEM((slots, width), jnp.bfloat16),
+            pltpu.VMEM((slots, width), jnp.bfloat16),
+            pltpu.VMEM((slots, width), jnp.bfloat16),
+            pltpu.VMEM((slots, width), jnp.bfloat16),
+            pltpu.VMEM((slots, rows_dev), jnp.bfloat16),
+            pltpu.VMEM((1, slots), jnp.int32),
+            pltpu.VMEM((peers, 1, slots), jnp.int32),
+            pltpu.SemaphoreType.DMA,
+            sems, sems, sems, sems, sems, sems,
+        ],
+        compiler_params=pltpu.CompilerParams(
+            collective_id=0, has_side_effects=True, vmem_limit_bytes=32 * 1024 * 1024
+        ),
+    )(embeddings, cluster_ids.reshape(1, rows_dev), owner.reshape(1, -1))
+
+
+def shards(embeddings, cluster_ids, owner):
+    slot = 2 * embeddings.shape[0] // lax.axis_size("dp")
+    if slot % ROW_TILE == 0:
+        return by_kernel(embeddings, cluster_ids, owner)
+    return by_collectives(embeddings, cluster_ids, owner)
+
+
 def solution(mesh):
     placed = (P(("groups", "dp"), None), P(("groups", "dp")), P("groups"))
     return jax.shard_map(

time: 58.2 us -> 36 us (0.62)
  Pallas kernels: 0 us -> 33.5 us
  waiting for transfers between devices: 31.6 us -> 0 us
  starting transfers between devices: 15 us -> 0 us
  local copies, waits for them, and re-layouts: 7.47 us -> 2.34 us
  other arithmetic: 2.15 us -> 0 us
  matrix products: 1.49 us -> 0 us
    pallas_call x0 -> x1, Pallas kernels: none -> 33.5 us  [by_kernel(): pl.pallas_call(functools.partial(smooth_kernel, peers, slot), out_shape=j...]
    all_to_all x3 -> x0, waiting for transfers between devices: 31.6 us -> none  [the longest x1 14.5 us: shards(): back = lax.all_to_all(result, 'dp', split_axis=0, concat_axis=0, tiled=True)]
    all_to_all x3 -> x0, starting transfers between devices: 15 us -> none  [the longest x1 7.39 us: shards(): lax.all_to_all(labels, 'dp', split_axis=0, concat_axis=0, tiled=True)]
    scatter x2 -> x0, local copies, waits for them, and re-layouts: 3.35 us -> none  [the longest x1 2.37 us: shards(): outgoing = jnp.zeros((peers * slot, width), jnp.bfloat16).at[target].set(...]
    gather x2 -> x0, local copies, waits for them, and re-layouts: 2.83 us -> none  [the longest x1 1.56 us: shards(): return back.reshape(-1, width)[target]]
    unnamed x4 -> x7, local copies, waits for them, and re-layouts: 0.01 us -> 2.34 us
    dot_general x2 -> x0, matrix products: 1.49 us -> none  [the longest x1 1.12 us: kernel_terms(): jnp.dot(affinity_factor.astype(jnp.bfloat16), key_rows, preferred_element...]
    all_to_all x2 -> x0, local copies, waits for them, and re-layouts: 1.2 us -> none  [shards(): lax.all_to_all(labels, 'dp', split_axis=0, concat_axis=0, tiled=True)]
  transfers between devices with their start and end apart: 3 -> 0, of which waited for: 3 -> 0; matrix products, arithmetic and copies ran while one was open for 6% -> 0% of each run, Pallas kernels for 0% -> 0%
where the time goes in v1:
time: 36 us; the launch traced here: 35.9 us
  Pallas kernels  33.5 us (93%)
  local copies, waits for them, and re-layouts  2.34 us (6%)
    pallas_call x1, Pallas kernels, by_kernel(): pl.pallas_call(functools.partial(smooth_kernel, peers, slot), out_shape=j...  33.5 us
    unnamed x7, local copies, waits for them, and re-layouts  2.34 us

profile of v1, /device:TPU:0, one launch (start us, length us, event | category | flops | bytes accessed | tf_op | source)
XLA Modules:
  0.0 35.9 jit_solution(2633381595088136986)
XLA Ops:
  0.0 0.0 copy-start.1
  0.0 0.0 copy-start.2
  0.0 0.7 %copy-done.1 = s32[512]{0:T(512)S(1)} copy-done((s32[512]{0:T(512)S(1)}, s32[512]{0:T(512)}, u32[]{:S(2)}) %copy-start.1) | copy-done | bytes 2072
  0.7 0.0 copy-done.2
  0.7 0.0 copy-start
  0.7 0.9 %copy-done = bf16[128,1024]{1,0:T(8,128)(2,1)S(1)} copy-done((bf16[128,1024]{1,0:T(8,128)(2,1)S(1)}, bf16[128,1024]{1,0:T(8,128)(2,1)}, u32[]{:S(2)}) %copy-start) | copy-done | bytes 262168
  1.6 33.5 %shard_map.37 = bf16[128,1024]{1,0:T(8,128)(2,1)S(1)} custom-call(bf16[128,1024]{1,0:T(8,128)(2,1)S(1)} %copy-done, s32[1,128]{1,0:T(1,128)S(1)} %bitcast.3, s32[1,512]{1,0:T(1,128)S(1)} %bitcast.2), custom_call_target="tpu_custom_call" | custom-call | tf_op jit(solution)/shard_map/pallas_call | solution.py:209
  35.2 0.7 %copy.5 = bf16[128,1024]{1,0:T(8,128)(2,1)} copy(bf16[128,1024]{1,0:T(8,128)(2,1)S(1)} %shard_map.37) | data formatting | bytes 524288
Async XLA Ops:
  0.0 0.7 %copy-start.1 = (s32[512]{0:T(512)S(1)}, s32[512]{0:T(512)}, u32[]{:S(2)}) copy-start(s32[512]{0:T(512)} %param.5) | copy-start | bytes 6148
  0.0 0.7 %copy-start.2 = (s32[128]{0:T(128)S(1)}, s32[128]{0:T(128)}, u32[]{:S(2)}) copy-start(s32[128]{0:T(128)} %param.4) | copy-start | bytes 1540
  0.7 1.0 %copy-start = (bf16[128,1024]{1,0:T(8,128)(2,1)S(1)}, bf16[128,1024]{1,0:T(8,128)(2,1)}, u32[]{:S(2)}) copy-start(bf16[128,1024]{1,0:T(8,128)(2,1)} %emb_hbm.1) | copy-start | bytes 786436

commit v2 on v1

--- a/solution.py
+++ b/solution.py
@@ -94,7 +94,7 @@
             device_id_type=pl.DeviceIdType.MESH,
         )
 
-    order = sorted(range(1, peers), key=lambda k: abs(k - peers // 2))
+    order = sorted(range(1, peers), key=lambda k: -abs(k - peers // 2))
 
     def remote(src, dst, send, recv, k, forward):
         peer = lax.rem(me + (k if forward else peers - k), peers)
@@ -142,7 +142,7 @@
     lab_in[0] = labels
 
     far = slice(slots // 4, 3 * slots // 4)
-    groups = [far, slice(0, slots // 4), slice(3 * slots // 4, slots)]
+    groups = [slice(0, slots // 4), slice(3 * slots // 4, slots), far]
 
     def inside(part):
         return [k for k in order if part.start <= k * slot < part.stop]
@@ -170,7 +170,7 @@
     label_col = jnp.sum(jnp.where(square, label_row, 0), axis=1, keepdims=True)
     same = label_col == label_row
 
-    for k in reversed(order):
+    for k in order:
         row_copy[k].wait_recv()
         here = slice(k * slot, (k + 1) * slot)
         unit[here, :] = normalize(got[here, :])
@@ -179,24 +179,28 @@
         unit[...], unit[...], (((1,), (1,)), ((), ())), preferred_element_type=jnp.float32
     )
     weight = jnp.where(same, jnp.exp((gram - 1.0) / sharpness_scale), 0.0)
-    total = jnp.sum(weight, axis=1, keepdims=True)
+    inverse = 1.0 / jnp.sum(weight, axis=1, keepdims=True)
     weight_b = weight.astype(jnp.bfloat16)
     for part in groups:
         numer = jnp.dot(weight_b[part], got[...], preferred_element_type=jnp.float32)
-        made[part, :] = (numer / total[part]).astype(jnp.bfloat16)
+        made[part, :] = (numer * inverse[part]).astype(jnp.bfloat16)
         for k in inside(part):
             back_copy[k].start()
     back[:slot, :] = made[:slot, :]
 
-    for k in reversed(order):
-        back_copy[k].wait_recv()
-    out_ref[...] = lax.dot_general(
-        place[...], back[...], (((0,), (0,)), ((), ())), preferred_element_type=jnp.float32
-    ).astype(out_ref.dtype)
     for k in order:
         lab_copy[k].wait_send()
         row_copy[k].wait_send()
-        back_copy[k].wait_send()
+    rows = jnp.zeros((rows_dev, width), jnp.float32)
+    for part in groups:
+        for k in inside(part):
+            back_copy[k].wait_send()
+            back_copy[k].wait_recv()
+        rows += lax.dot_general(
+            place[part, :], back[part, :], (((0,), (0,)), ((), ())),
+            preferred_element_type=jnp.float32,
+        )
+    out_ref[...] = rows.astype(out_ref.dtype)
 
 
 def by_kernel(embeddings, cluster_ids, owner):

time: 36 us -> 34 us (0.944)
  the two profiles are of different devices: /device:TPU:0 before, /device:TPU:5 now
where the time goes in v2:
time: 34 us; the launch traced here: 33.8 us
  Pallas kernels  31.5 us (93%)
  local copies, waits for them, and re-layouts  2.34 us (7%)
    pallas_call x1, Pallas kernels, by_kernel(): pl.pallas_call(functools.partial(smooth_kernel, peers, slot), out_shape=j...  31.5 us
    unnamed x7, local copies, waits for them, and re-layouts  2.34 us

profile of v2, /device:TPU:5, one launch (start us, length us, event | category | flops | bytes accessed | tf_op | source)
XLA Modules:
  0.0 33.8 jit_solution(7435510791779998050)
XLA Ops:
  0.0 0.0 copy-start.1
  0.0 0.0 copy-start.2
  0.0 0.7 %copy-done.1 = s32[512]{0:T(512)S(1)} copy-done((s32[512]{0:T(512)S(1)}, s32[512]{0:T(512)}, u32[]{:S(2)}) %copy-start.1) | copy-done | bytes 2072
  0.7 0.0 copy-done.2
  0.7 0.0 copy-start
  0.7 0.9 %copy-done = bf16[128,1024]{1,0:T(8,128)(2,1)S(1)} copy-done((bf16[128,1024]{1,0:T(8,128)(2,1)S(1)}, bf16[128,1024]{1,0:T(8,128)(2,1)}, u32[]{:S(2)}) %copy-start) | copy-done | bytes 262168
  1.6 31.5 %shard_map.37 = bf16[128,1024]{1,0:T(8,128)(2,1)S(1)} custom-call(bf16[128,1024]{1,0:T(8,128)(2,1)S(1)} %copy-done, s32[1,128]{1,0:T(1,128)S(1)} %bitcast.3, s32[1,512]{1,0:T(1,128)S(1)} %bitcast.2), custom_call_target="tpu_custom_call" | custom-call | tf_op jit(solution)/shard_map/pallas_call | solution.py:213
  33.1 0.7 %copy.5 = bf16[128,1024]{1,0:T(8,128)(2,1)} copy(bf16[128,1024]{1,0:T(8,128)(2,1)S(1)} %shard_map.37) | data formatting | bytes 524288
Async XLA Ops:
  0.0 0.7 %copy-start.1 = (s32[512]{0:T(512)S(1)}, s32[512]{0:T(512)}, u32[]{:S(2)}) copy-start(s32[512]{0:T(512)} %param.5) | copy-start | bytes 6148
  0.0 0.7 %copy-start.2 = (s32[128]{0:T(128)S(1)}, s32[128]{0:T(128)}, u32[]{:S(2)}) copy-start(s32[128]{0:T(128)} %param.4) | copy-start | bytes 1540
  0.7 1.0 %copy-start = (bf16[128,1024]{1,0:T(8,128)(2,1)S(1)}, bf16[128,1024]{1,0:T(8,128)(2,1)}, u32[]{:S(2)}) copy-start(bf16[128,1024]{1,0:T(8,128)(2,1)} %emb_hbm.1) | copy-start | bytes 786436

commit v3 on v2

--- a/solution.py
+++ b/solution.py
@@ -141,8 +141,8 @@
     lab_out[...] = labels
     lab_in[0] = labels
 
-    far = slice(slots // 4, 3 * slots // 4)
-    groups = [slice(0, slots // 4), slice(3 * slots // 4, slots), far]
+    quarter = slots // 4
+    groups = [slice(i * quarter, (i + 1) * quarter) for i in (0, 3, 1, 2)]
 
     def inside(part):
         return [k for k in order if part.start <= k * slot < part.stop]

time: 34 us -> 33.2 us (0.976)
  the two profiles are of different devices: /device:TPU:5 before, /device:TPU:1 now
where the time goes in v3:
time: 33.2 us; the launch traced here: 33 us
  Pallas kernels  30.7 us (92%)
  local copies, waits for them, and re-layouts  2.34 us (7%)
    pallas_call x1, Pallas kernels, by_kernel(): pl.pallas_call(functools.partial(smooth_kernel, peers, slot), out_shape=j...  30.7 us
    unnamed x7, local copies, waits for them, and re-layouts  2.34 us

profile of v3, /device:TPU:1, one launch (start us, length us, event | category | flops | bytes accessed | tf_op | source)
XLA Modules:
  0.0 33.0 jit_solution(10501070888494114603)
XLA Ops:
  0.0 0.0 copy-start.1
  0.0 0.0 copy-start.2
  0.0 0.7 %copy-done.1 = s32[512]{0:T(512)S(1)} copy-done((s32[512]{0:T(512)S(1)}, s32[512]{0:T(512)}, u32[]{:S(2)}) %copy-start.1) | copy-done | bytes 2072
  0.7 0.0 copy-done.2
  0.7 0.0 copy-start
  0.7 0.9 %copy-done = bf16[128,1024]{1,0:T(8,128)(2,1)S(1)} copy-done((bf16[128,1024]{1,0:T(8,128)(2,1)S(1)}, bf16[128,1024]{1,0:T(8,128)(2,1)}, u32[]{:S(2)}) %copy-start) | copy-done | bytes 262168
  1.6 30.7 %shard_map.37 = bf16[128,1024]{1,0:T(8,128)(2,1)S(1)} custom-call(bf16[128,1024]{1,0:T(8,128)(2,1)S(1)} %copy-done, s32[1,128]{1,0:T(1,128)S(1)} %bitcast.3, s32[1,512]{1,0:T(1,128)S(1)} %bitcast.2), custom_call_target="tpu_custom_call" | custom-call | tf_op jit(solution)/shard_map/pallas_call | solution.py:213
  32.3 0.7 %copy.5 = bf16[128,1024]{1,0:T(8,128)(2,1)} copy(bf16[128,1024]{1,0:T(8,128)(2,1)S(1)} %shard_map.37) | data formatting | bytes 524288
Async XLA Ops:
  0.0 0.7 %copy-start.1 = (s32[512]{0:T(512)S(1)}, s32[512]{0:T(512)}, u32[]{:S(2)}) copy-start(s32[512]{0:T(512)} %param.5) | copy-start | bytes 6148
  0.0 0.7 %copy-start.2 = (s32[128]{0:T(128)S(1)}, s32[128]{0:T(128)}, u32[]{:S(2)}) copy-start(s32[128]{0:T(128)} %param.4) | copy-start | bytes 1540
  0.7 1.0 %copy-start = (bf16[128,1024]{1,0:T(8,128)(2,1)S(1)}, bf16[128,1024]{1,0:T(8,128)(2,1)}, u32[]{:S(2)}) copy-start(bf16[128,1024]{1,0:T(8,128)(2,1)} %emb_hbm.1) | copy-start | bytes 786436
